TPU v7x, 32 devices: a whole 2x2x4 slice. The times are simulated.
32 devices in a mesh: pole: 2 (over y), prow: 1, pcol: 16 (over z, x, core).
Axes of the slice: x: 2, y: 2, z: 4, core: 2. Of those that a mesh axis runs over, the one named last changes fastest.
Arguments:
- anc_inverse: float32 [12288, 6144], P(('pole', 'prow'), 'pcol'), parts along dimension 0, may hold values from -8 to 8
- anc_factor: float32 [12288, 768], P(('pole', 'pcol')), parts along dimension 0, may hold values from -0.078125 to 0.078125
- win_factor: float32 [1536, 768], P('pole'), parts along dimension 0, may hold values from -0.375 to 0.375
- pivot_inverse: float32 [6, 256, 256], P('pole'), parts along dimension 0, may hold values from -6 to 6
- structure: int32 [3, 24], replicated, may hold values 0 or 1
Outputs:
- anc_columns: float32 [12288, 768], P(('pole', 'prow', 'pcol')), parts along dimension 0
- win_inverse: float32 [1536, 768], P('pole'), parts along dimension 0
There are 2 independent parts, one for each index of `pole`. A program takes and returns all parts, laid end to end along the dimension named above; an argument that names none is the same for every part. Nothing has to cross between parts.
All inputs are finite; a program needn't handle non-finite values.
Results may differ from a plain program's by a relative error of at most 0.0001.
Values sent between devices are 32-bit elements; how exact they have to be, the bound alone decides.
A program may use at most 128 MiB of HBM per device.

v0:
```python
import jax
import jax.numpy as jnp
from jax import lax
from jax.sharding import PartitionSpec as P

precise = lax.Precision.HIGHEST


def product(left, right):
    return jnp.dot(left, right, precision=precise, preferred_element_type=jnp.float32)


def on_device(anc_inverse, anc_factor, win_factor, pivot_inverse, structure):
    row_count = lax.axis_size("prow")
    col_count = lax.axis_size("pcol")
    row_index = lax.axis_index("prow")
    col_index = lax.axis_index("pcol")
    block_rows = anc_inverse.shape[0]
    block_cols = anc_inverse.shape[1]
    steps_total = pivot_inverse.shape[0]
    width = pivot_inverse.shape[1]
    all_cols = anc_factor.shape[1]
    block_count = structure.shape[1]
    ratio_cols = col_count // row_count
    share_rows = block_rows // col_count
    structure_cols = structure.T.astype(jnp.float32)
    global_rows = col_index * block_cols + lax.iota(jnp.int32, block_cols)
    onehot_rows = (
        (global_rows // width)[:, None] == lax.iota(jnp.int32, block_count)[None, :]
    ).astype(jnp.float32)
    kept_rows = product(onehot_rows, structure_cols)
    share_offset = col_index * share_rows
    share_global = (row_index * col_count + col_index) * share_rows + lax.iota(
        jnp.int32, share_rows
    )
    onehot_share = (
        (share_global // width)[:, None] == lax.iota(jnp.int32, block_count)[None, :]
    ).astype(jnp.float32)
    kept_share = product(onehot_share, structure_cols)
    slot_ids = lax.iota(jnp.int32, col_count)
    source_flag = (slot_ids // row_count == col_index - row_index * ratio_cols).astype(jnp.float32)
    pieces = jnp.tile(anc_factor.reshape(row_count, share_rows, all_cols), (ratio_cols, 1, 1))
    outgoing = pieces * source_flag[:, None, None]
    incoming = lax.all_to_all(outgoing, "pcol", split_axis=0, concat_axis=0, tiled=True)
    factor_share = jnp.sum(incoming, axis=0)
    column_store = {}
    share_store = {}
    window_blocks = {}
    for k in range(steps_total - 1, -1, -1):
        first_col = k * width
        factor_now = anc_factor[:, first_col : first_col + width] * kept_rows[:, k : k + 1]
        share_factor = factor_share[:, first_col : first_col + width] * kept_share[:, k : k + 1]
        finished = list(range(k + 1, steps_total))
        if finished:
            stacked = jnp.concatenate([column_store[j] for j in finished], axis=1)
            factor_win = win_factor[first_col + width :, first_col : first_col + width]

        def term_rows(start, count, factor_now=factor_now):
            return product(anc_inverse, factor_now)

        share_image = lax.psum_scatter(
            term_rows(jnp.int32(0), share_rows * lax.axis_size("pcol")),
            "pcol",
            scatter_dimension=0,
            tiled=True,
        )
        if finished:
            share_image = share_image + product(
                lax.dynamic_slice_in_dim(stacked, share_offset, share_rows, 0), factor_win
            )
        share_column = -share_image
        column_now = lax.all_gather(share_column, "pcol", axis=0, tiled=True)
        crossings = [product(share_store[j].T, share_factor) for j in finished]
        pivot_part = product(share_factor.T, share_column)
        cross_sums = []
        if finished:
            cross_total = lax.psum(jnp.stack(crossings), ("prow", "pcol"))
            cross_sums = [cross_total[position] for position in range(len(finished))]
        pivot_sum = lax.psum(pivot_part, ("prow", "pcol"))
        for position, j in enumerate(finished):
            running = cross_sums[position]
            for i in finished:
                running = running + product(
                    window_blocks[j, i],
                    win_factor[i * width : (i + 1) * width, first_col : first_col + width],
                )
            window_blocks[j, k] = -running
            window_blocks[k, j] = -running.T
        pivot_block = pivot_inverse[k] - pivot_sum
        for j in finished:
            pivot_block = pivot_block - product(
                win_factor[j * width : (j + 1) * width, first_col : first_col + width].T,
                window_blocks[j, k],
            )
        window_blocks[k, k] = pivot_block
        column_store[k] = column_now
        share_store[k] = share_column
    anc_columns = jnp.concatenate([share_store[k] for k in range(steps_total)], axis=1)
    win_inverse = jnp.concatenate(
        [
            jnp.concatenate([window_blocks[i, k] for k in range(steps_total)], axis=1)
            for i in range(steps_total)
        ],
        axis=0,
    )
    return (anc_columns, win_inverse)


def solution(mesh):
    in_specs = (
        P(("pole", "prow"), "pcol"),
        P(("pole", "pcol"), None),
        P("pole", None),
        P("pole", None, None),
        P(),
    )
    out_specs = (P(("pole", "prow", "pcol"), None), P("pole", None))
    return jax.shard_map(
        on_device, mesh=mesh, in_specs=in_specs, out_specs=out_specs, check_vma=False
    )
```

profile of v0, /device:TPU:1, one launch (start us, length us, event | category | flops | bytes accessed | tf_op | source)
XLA Modules:
  0.0 903.5 jit_solution(14524148858973868540)
XLA Ops:
  7.2 0.0 reduce-scatter.8.cloned.1.call-start
  7.2 1.0 fusion.40
  8.2 19.4 %convolution_bitcast_fusion = f32[6144,256]{0,1:T(8,128)} fusion(f32[6144,384]{1,0:T(8,128)} %param.5, f32[384,768]{1,0:T(8,128)} %param.6, f32[384]{0:T(512)S(1)} %get-tuple-element.7), kind=kOutput, calls=%fused_computation.3 | convolution fusion | flops 7247855616 | bytes 16123392 | tf_op jit(solution)/shard_map/dot_general | solution.py:10
  27.6 0.2 reduce-scatter.6.cloned.1.call-start
  27.9 1.0 copy-done.2
  28.9 19.2 %convolution_bitcast_fusion.1 = f32[6144,256]{0,1:T(8,128)} fusion(f32[6144,384]{1,0:T(8,128)} %param.5, f32[384,768]{1,0:T(8,128)S(1)} %copy-done.2, f32[384]{0:T(512)S(1)} %get-tuple-element.8), kind=kOutput, calls=%fused_computation.4 | convolution fusion | flops 7247855616 | bytes 16123904 | tf_op jit(solution)/shard_map/dot_general | solution.py:10
  48.1 8.4 broadcast_multiply_fusion
  56.5 7.3 all-to-all-start
  63.8 346.6 %reduce-scatter.8.cloned.1.call-done = f32[384,256]{0,1:T(8,128)} async-done(((f32[6144,256]{0,1:T(8,128)}), f32[384,256]{0,1:T(8,128)}) %reduce-scatter.8.cloned.1.call-update) | async-done | bytes 393232 | tf_op jit(solution)/shard_map/reduce_scatter | solution.py:61
  410.5 1.8 neg.30
  412.2 0.3 reduce-scatter.4.cloned.1.call-start
  412.5 19.2 %convolution_bitcast_fusion.2 = f32[6144,256]{0,1:T(8,128)} fusion(f32[6144,384]{1,0:T(8,128)} %param.5, f32[384,768]{1,0:T(8,128)S(1)} %copy-done.2, f32[384]{0:T(512)S(1)} %get-tuple-element.6), kind=kOutput, calls=%fused_computation.5 | convolution fusion | flops 7247855616 | bytes 16123904 | tf_op jit(solution)/shard_map/dot_general | solution.py:10
  431.8 0.0 all-gather.5.cloned.1.call-start
  431.8 121.0 %reduce-scatter.6.cloned.1.call-done = f32[384,256]{0,1:T(8,128)} async-done(((f32[6144,256]{0,1:T(8,128)}), f32[384,256]{0,1:T(8,128)}) %reduce-scatter.6.cloned.1.call-update) | async-done | bytes 393232 | tf_op jit(solution)/shard_map/reduce_scatter | solution.py:61
  552.8 65.2 %all-gather.3.cloned.1.call-done = f32[6144,256]{0,1:T(8,128)} async-done(((f32[384,256]{0,1:T(8,128)}), f32[6144,256]{0,1:T(8,128)}) %all-gather.3.cloned.1.call-update) | async-done | bytes 6291472 | tf_op jit(solution)/shard_map/all_gather | solution.py:72
  617.9 2.6 fusion.1
  620.5 0.3 all-reduce.3.cloned.1.call-start
  620.9 83.5 %reduce-scatter.4.cloned.1.call-done = f32[384,256]{0,1:T(8,128)} async-done(((f32[6144,256]{0,1:T(8,128)}), f32[384,256]{0,1:T(8,128)}) %reduce-scatter.4.cloned.1.call-update) | async-done | bytes 393232 | tf_op jit(solution)/shard_map/reduce_scatter | solution.py:61
  704.4 65.1 %all-gather.5.cloned.1.call-done = f32[6144,256]{0,1:T(8,128)} async-done(((f32[384,256]{0,1:T(8,128)}), f32[6144,256]{0,1:T(8,128)}) %all-gather.5.cloned.1.call-update) | async-done | bytes 6291472 | tf_op jit(solution)/shard_map/all_gather | solution.py:72
  769.5 2.4 fusion
  771.9 7.7 reduce_sum.9
  779.6 0.9 convolution_bitcast_fusion.7
  780.5 1.4 fusion.20
  781.9 1.6 fusion.21
  783.5 0.9 convolution_bitcast_fusion.6
  784.4 0.8 pad_maximum_fusion.2
  785.2 1.4 fusion.19
  786.6 1.6 fusion.11
  788.2 0.8 copy.42
  789.0 0.1 pad_maximum_fusion
  789.1 1.4 copy.32
  790.5 91.5 %all-reduce.3.cloned.1.call-done = (f32[256,256]{1,0:T(8,128)}, f32[256,256]{1,0:T(8,128)}, f32[2,256,256]{1,2,0:T(8,128)}, f32[256,256]{0,1:T(8,128)}, f32[256,256]{1,0:T(8,128)}) async-done(((f32[256,256]{1,0:T(8,128)}, f32[256,256]{1,0:T(8,128)}, f32[2,256,256]{1,2,0:T(8,128)}, f32[256,256]{0,1:T(8,128)}, f32[256,256]{1,0:T(8,128)}), (f32[256,256]{1,0:T(8,128)}, f32[256,256]{1,0:T(8,128)}, ...) | async-done | bytes 1572880 | tf_op jit(solution)/shard_map/psum | solution.py:79
  882.0 1.1 bitcast_subtract_fusion
  883.1 1.4 fusion.7
  884.5 1.6 convolution_add_fusion.3
  886.2 1.5 fusion.6
  887.8 0.7 copy-done.5
  888.5 0.6 convolution_add_fusion.5
  889.1 0.6 fusion.5
  889.7 0.6 fusion.3
  890.3 0.8 copy.30
  891.1 1.7 fusion.4
  892.8 1.3 fusion.2
  894.1 0.1 pad_maximum_fusion.1
  894.2 0.3 copy.31
  894.4 0.6 copy-done.8
  895.1 0.1 copy-done.9
  895.1 1.6 maximum_maximum_fusion
  (31 shorter events, 0.2 us)
Async XLA Ops:
  7.2 403.3 %reduce-scatter.8.cloned.1.call-start = ((), (), s32[]{:S(2)}) async-start(), calls=%async_computation.6 | async-start | bytes 6684672 | tf_op jit(solution)/shard_map/reduce_scatter | solution.py:61
  27.6 1.3 copy-start.2
  27.6 525.2 %reduce-scatter.6.cloned.1.call-start = ((), (), s32[]{:S(2)}) async-start(), calls=%async_computation.5 | async-start | bytes 6684672 | tf_op jit(solution)/shard_map/reduce_scatter | solution.py:61
  56.5 715.4 %all-to-all-start = ((f32[16,384,768]{2,1,0:T(8,128)}), f32[16,384,768]{2,1,0:T(8,128)}, u32[]{:S(2)}, u32[]{:S(2)}) async-start(f32[16,384,768]{2,1,0:T(8,128)} %broadcast_multiply_fusion), calls=%async_computation.3 | async-start | bytes 37748736 | tf_op jit(solution)/shard_map/all_to_all | solution.py:44
  63.8 554.2 %all-gather.3.cloned.1.call-start = ((), (), s32[]{:S(2)}) async-start(), calls=%async_computation.7 | async-start | bytes 6684672 | tf_op jit(solution)/shard_map/all_gather | solution.py:72
  412.2 292.1 %reduce-scatter.4.cloned.1.call-start = ((), (), s32[]{:S(2)}) async-start(), calls=%async_computation.4 | async-start | bytes 6684672 | tf_op jit(solution)/shard_map/reduce_scatter | solution.py:61
  431.8 337.7 %all-gather.5.cloned.1.call-start = ((), (), s32[]{:S(2)}) async-start(), calls=%async_computation.8 | async-start | bytes 6684672 | tf_op jit(solution)/shard_map/all_gather | solution.py:72
  620.5 261.5 %all-reduce.3.cloned.1.call-start = ((), (), s32[]{:S(2)}) async-start(), calls=%async_computation.9 | async-start | bytes 3145728 | tf_op jit(solution)/shard_map/psum | solution.py:79
  771.9 7.7 copy-start
  779.6 3.9 copy-start.1
  785.2 3.0 slice-start
  785.2 3.8 copy-start.3
  790.5 95.7 %copy-start.4 = (f32[768,768]{1,0:T(8,128)S(1)}, f32[768,768]{1,0:T(8,128)}, u32[]{:S(2)}) copy-start(f32[768,768]{1,0:T(8,128)} %param.7) | copy-start | bytes 7077892
  790.5 95.7 %copy-start.7 = (f32[1,256,256]{1,2,0:T(8,128)S(1)}, f32[1,256,256]{1,2,0:T(8,128)}, u32[]{:S(2)}) copy-start(f32[1,256,256]{1,2,0:T(8,128)} %copy.42) | copy-start | bytes 786436
  882.0 6.5 copy-start.10
  887.8 0.7 copy-start.5
  891.1 3.0 copy-start.6
  894.1 0.9 copy-start.8
  894.1 1.0 copy-start.9
Sparse Core Ops, SparseCore 0:
  27.8 382.6 reduce-scatter.7
  414.9 137.8 reduce-scatter.5
  555.7 62.2 all-gather.2
  621.7 82.6 reduce-scatter.3
  707.4 62.0 all-gather.4
  788.3 93.6 all-reduce.2
where the time goes:
time: 906 us; the launch traced here: 904 us
  waiting for transfers between devices  773 us (85%)
  matrix products  80.8 us (9%)
  other arithmetic  21.5 us (2%)
  between operations  14.3 us (2%)
    reduce_scatter x3, waiting for transfers between devices, on_device(): lax.psum_scatter(term_rows(jnp.int32(0), share_rows * lax.axis_size('pcol...  551 us
    all_gather x2, waiting for transfers between devices, on_device(): column_now = lax.all_gather(share_column, 'pcol', axis=0, tiled=True)  130 us
    psum x1, waiting for transfers between devices, on_device(): pivot_sum = lax.psum(pivot_part, ('prow', 'pcol'))  91.5 us
    dot_general x20, matrix products, product(): jnp.dot(left, right, precision=precise, preferred_element_type=jnp.float32)  80.8 us
  transfers between devices with their start and end apart: 7, of which 6 were waited for; matrix products, arithmetic and copies ran while one was open for 6% of the time, Pallas kernels for 0%

commit v1 on v0

--- a/solution.py
+++ b/solution.py
@@ -1,7 +1,373 @@
+import functools
+
 import jax
 import jax.numpy as jnp
 from jax import lax
+from jax.experimental import pallas as pl
+from jax.experimental.pallas import tpu as pltpu
 from jax.sharding import PartitionSpec as P
+
+MESH = pl.DeviceIdType.MESH
+UP, DOWN, ACROSS, MATE = range(4)
+Z = 4
+LANES = 8
+
+
+def split(value):
+    high = value.astype(jnp.bfloat16)
+    low = (value - high.astype(jnp.float32)).astype(jnp.bfloat16)
+    return high, low
+
+
+def dot3(left, right):
+    (lh, ll), (rh, rl) = left, right
+    dot = functools.partial(jnp.dot, preferred_element_type=jnp.float32)
+    return dot(lh, rh) + (dot(lh, rl) + dot(ll, rh))
+
+
+def mul(left, right):
+    return dot3(split(left), split(right))
+
+
+def fused_kernel(steps, width, anc_ref, fac_ref, win_ref, piv_ref, str_ref, cols_ref, out_ref, *scratch):
+    (gath, fac_st, anc_st, win_st, piv_st, tr_hi, tr_lo, acc, pivot_rest) = scratch[:9]
+    parts = scratch[9 : 9 + steps]
+    mates = scratch[9 + steps : 9 + 2 * steps]
+    halves = scratch[9 + 2 * steps : 9 + 3 * steps]
+    slots = scratch[9 + 3 * steps : 9 + 4 * steps]
+    sums = scratch[9 + 4 * steps : 9 + 5 * steps]
+    (load_sem, send_sem, recv_sem, s1, r1, s2, r2, s3, r3, s4, r4) = scratch[9 + 5 * steps :]
+
+    me = lax.axis_index("pcol")
+    core = lax.rem(me, 2)
+    x = lax.rem(me // 2, 2)
+    z = me // 4
+    lane = me // 2
+    rows = fac_st.shape[0]
+    half = width // 2
+    piece = half // LANES
+    mate = me + 1 - 2 * core
+
+    def index(zz, xx, cc):
+        return (zz * 2 + xx) * 2 + cc
+
+    across = index(z, 1 - x, core)
+
+    load_fac = pltpu.make_async_copy(fac_ref, fac_st, load_sem.at[0])
+    load_anc = pltpu.make_async_copy(anc_ref, anc_st, load_sem.at[1])
+    load_win = pltpu.make_async_copy(win_ref, win_st, load_sem.at[2])
+    load_piv = pltpu.make_async_copy(piv_ref, piv_st, load_sem.at[3])
+    load_fac.start()
+
+    barrier = pltpu.get_barrier_semaphore()
+    for d in range(1, LANES):
+        peer = lax.rem(lane + d, LANES) * 2 + core
+        pl.semaphore_signal(barrier, inc=1, device_id={"pcol": peer}, device_id_type=MESH)
+    pl.semaphore_signal(barrier, inc=1, device_id={"pcol": mate}, device_id_type=MESH)
+
+    load_fac.wait()
+    load_anc.start()
+    load_win.start()
+    load_piv.start()
+    sub = width // 2
+
+    def mask_own(k):
+        for piece_at in range(rows // sub):
+            block = (me * (rows // sub) + piece_at) // 2
+            kept = str_ref[k, block].astype(jnp.float32)
+            gath[k, me, piece_at * sub : (piece_at + 1) * sub, :] = (
+                fac_st[piece_at * sub : (piece_at + 1) * sub, k * width : (k + 1) * width] * kept
+            )
+
+    mask_own(steps - 1)
+    pl.semaphore_wait(barrier, LANES)
+
+    def remote(kind, k, block, dest):
+        return pltpu.make_async_remote_copy(
+            src_ref=gath.at[k, block],
+            dst_ref=gath.at[k, block],
+            send_sem=send_sem.at[kind, k, block],
+            recv_sem=recv_sem.at[k, block],
+            device_id={"pcol": dest},
+            device_id_type=MESH,
+        )
+
+    def order(t):
+        inner = (0, 0, 2, 3) if t else (1, 1, 1, 1)
+        lowmid = inner[t] if t else 1
+        highmid = 3 - lowmid
+        return jnp.where(z == 0, t, jnp.where(z == 1, lowmid, jnp.where(z == 2, highmid, 3 - t)))
+
+    def column_sends(k, t, act):
+        zz = order(t)
+        block = index(zz, x, core)
+
+        def vertical(kind, dest, cond):
+            @pl.when(cond)
+            def _():
+                act(remote(kind, k, block, dest))
+
+        if t == 0:
+            vertical(UP, jnp.minimum(me + 4, 4 * Z - 1), z < Z - 1)
+            vertical(DOWN, jnp.maximum(me - 4, 0), z > 0)
+        else:
+            vertical(UP, jnp.minimum(me + 4, 4 * Z - 1), (zz < z) & (z < Z - 1))
+            vertical(DOWN, jnp.maximum(me - 4, 0), (zz > z) & (z > 0))
+        act(remote(ACROSS, k, block, across))
+        act(remote(MATE, k, block, mate))
+
+    def arrived(k, block):
+        remote(MATE, k, block, mate).wait_recv()
+
+    def column_event(k, t):
+        if t > 0:
+            arrived(k, index(order(t), x, core))
+        column_sends(k, t, lambda copy: copy.start())
+
+    def across_event(k, t):
+        block = index(order(t), 1 - x, core)
+        arrived(k, block)
+        remote(MATE, k, block, mate).start()
+
+    def compute_event(k, t):
+        zz = order(t)
+        arrived(k, index(zz, x, 1 - core))
+        arrived(k, index(zz, 1 - x, 1 - core))
+
+        def body(i, carry):
+            block = zz * 4 + i
+            if k == steps - 1:
+                tile = anc_st[pl.ds(pl.multiple_of(block * rows, rows), rows), :].T
+                high, low = split(tile)
+                tr_hi[block] = high
+                tr_lo[block] = low
+            else:
+                high, low = tr_hi[block], tr_lo[block]
+            term = dot3((high, low), split(gath[k, block]))
+            acc[...] += term
+            return carry
+
+        if t == 0:
+            acc[...] = jnp.zeros_like(acc)
+        lax.fori_loop(0, 4, body, 0)
+
+    def fac_block(j, k):
+        return win_st[j * width : (j + 1) * width, k * width : (k + 1) * width]
+
+    def finish(k):
+        total = acc[...]
+        for j in range(k + 1, steps):
+            total = total + mul(cols_ref[:, j * width : (j + 1) * width], fac_block(j, k))
+        column = -total
+        cols_ref[:, k * width : (k + 1) * width] = column
+        flipped = split(column.T)
+        for i in range(k + 1):
+            parts[k][:, i * width : (i + 1) * width] = dot3(flipped, split(gath[i, me]))
+
+    def mate_copy(k):
+        return pltpu.make_async_remote_copy(
+            src_ref=parts[k].at[pl.ds(pl.multiple_of((1 - core) * half, half), half), :],
+            dst_ref=mates[k],
+            send_sem=s1.at[k],
+            recv_sem=r1.at[k],
+            device_id={"pcol": mate},
+            device_id_type=MESH,
+        )
+
+    def scatter_copy(k, d):
+        peer = lax.rem(lane + d, LANES)
+        return pltpu.make_async_remote_copy(
+            src_ref=halves[k].at[pl.ds(pl.multiple_of(peer * piece, piece), piece), :],
+            dst_ref=slots[k].at[lane],
+            send_sem=s2.at[k, peer],
+            recv_sem=r2.at[k, lane],
+            device_id={"pcol": peer * 2 + core},
+            device_id_type=MESH,
+        )
+
+    def scatter_wait(k, d):
+        peer = lax.rem(lane + d, LANES)
+        pltpu.make_async_remote_copy(
+            src_ref=slots[k].at[peer],
+            dst_ref=slots[k].at[peer],
+            send_sem=s2.at[k, peer],
+            recv_sem=r2.at[k, peer],
+            device_id={"pcol": peer * 2 + core},
+            device_id_type=MESH,
+        ).wait_recv()
+
+    def spread_copy(k, d, owner):
+        peer = lax.rem(lane + d, LANES)
+        at = pl.ds(pl.multiple_of(core * half + owner * piece, piece), piece)
+        return pltpu.make_async_remote_copy(
+            src_ref=sums[k].at[at, :],
+            dst_ref=sums[k].at[at, :],
+            send_sem=s3.at[k, peer],
+            recv_sem=r3.at[k, owner],
+            device_id={"pcol": peer * 2 + core},
+            device_id_type=MESH,
+        )
+
+    def join_copy(k, which):
+        at = pl.ds(pl.multiple_of(which * half, half), half)
+        return pltpu.make_async_remote_copy(
+            src_ref=sums[k].at[at, :],
+            dst_ref=sums[k].at[at, :],
+            send_sem=s4.at[k],
+            recv_sem=r4.at[k],
+            device_id={"pcol": mate},
+            device_id_type=MESH,
+        )
+
+    def phase(k, number):
+        if number == 1:
+            mate_copy(k).start()
+        elif number == 2:
+            mate_copy(k).wait_recv()
+            own = pl.ds(pl.multiple_of(core * half, half), half)
+            halves[k][...] = parts[k][own, :] + mates[k][...]
+            for d in range(1, LANES):
+                scatter_copy(k, d).start()
+        elif number == 3:
+            total = halves[k][pl.ds(pl.multiple_of(lane * piece, piece), piece), :]
+            for d in range(1, LANES):
+                scatter_wait(k, d)
+                total = total + slots[k][lax.rem(lane + d, LANES)]
+            sums[k][pl.ds(pl.multiple_of(core * half + lane * piece, piece), piece), :] = total
+            for d in range(1, LANES):
+                spread_copy(k, d, lane).start()
+        elif number == 4:
+            for d in range(1, LANES):
+                spread_copy(k, d, lax.rem(lane + d, LANES)).wait_recv()
+            join_copy(k, core).start()
+        else:
+            join_copy(k, 1 - core).wait_recv()
+            window(k)
+
+    def put(j, k, value):
+        out_ref[j * width : (j + 1) * width, k * width : (k + 1) * width] = value
+
+    def got(j, k):
+        return out_ref[j * width : (j + 1) * width, k * width : (k + 1) * width]
+
+    def summed(j, k):
+        return sums[j][:, k * width : (k + 1) * width]
+
+    def window(k):
+        if k == 0:
+            put(0, 0, pivot_rest[...] - summed(0, 0).T)
+            return
+        diag = piv_st[k] - summed(k, k).T
+        for j in range(k + 1, steps):
+            diag = diag - mul(fac_block(j, k).T, got(j, k))
+        put(k, k, diag)
+        low = k - 1
+        for j in range(k, steps):
+            running = summed(j, low)
+            for i in range(k, steps):
+                running = running + mul(got(j, i), fac_block(i, low))
+            put(j, low, -running)
+            put(low, j, -running.T)
+        if low == 0:
+            rest = piv_st[0]
+            for j in range(1, steps):
+                rest = rest - mul(fac_block(j, 0).T, got(j, 0))
+            pivot_rest[...] = rest
+
+    events = [(k, t) for k in range(steps - 1, -1, -1) for t in range(Z)]
+    lag_across, lag_compute = 1, 2
+    pending = []
+    for g in range(len(events) + lag_compute):
+        if g < len(events):
+            column_event(*events[g])
+        if g == 0:
+            for k in range(steps - 1):
+                mask_own(k)
+            load_anc.wait()
+            load_win.wait()
+            load_piv.wait()
+        if 0 <= g - lag_across < len(events):
+            across_event(*events[g - lag_across])
+        for k, first in pending:
+            number = g - first + 1
+            if 2 <= number <= 5:
+                phase(k, number)
+        if g >= lag_compute:
+            k, t = events[g - lag_compute]
+            compute_event(k, t)
+            if t == Z - 1:
+                finish(k)
+                phase(k, 1)
+                pending.append((k, g))
+    for g in range(len(events) + lag_compute, len(events) + lag_compute + 4):
+        for k, first in pending:
+            number = g - first + 1
+            if 2 <= number <= 5:
+                phase(k, number)
+
+    for k, t in events:
+        column_sends(k, t, lambda copy: copy.wait_send())
+        remote(MATE, k, index(order(t), 1 - x, core), mate).wait_send()
+    for k in range(steps):
+        mate_copy(k).wait_send()
+        for d in range(1, LANES):
+            scatter_copy(k, d).wait_send()
+            spread_copy(k, d, lane).wait_send()
+        join_copy(k, core).wait_send()
+
+
+def fused(anc_inverse, anc_factor, win_factor, pivot_inverse, structure):
+    steps, width = pivot_inverse.shape[:2]
+    rows, all_cols = anc_factor.shape
+    devices = lax.axis_size("pcol")
+    half = width // 2
+    piece = half // LANES
+    f32, b16 = jnp.float32, jnp.bfloat16
+    wide = [(k + 1) * width for k in range(steps)]
+    dma = pltpu.SemaphoreType.DMA
+    scratch = [
+        pltpu.VMEM((steps, devices, rows, width), f32),
+        pltpu.VMEM((rows, all_cols), f32),
+        pltpu.VMEM(anc_inverse.shape, f32),
+        pltpu.VMEM(win_factor.shape, f32),
+        pltpu.VMEM(pivot_inverse.shape, f32),
+        pltpu.VMEM((devices, rows, rows), b16),
+        pltpu.VMEM((devices, rows, rows), b16),
+        pltpu.VMEM((rows, width), f32),
+        pltpu.VMEM((width, width), f32),
+        *[pltpu.VMEM((width, w), f32) for w in wide],
+        *[pltpu.VMEM((half, w), f32) for w in wide],
+        *[pltpu.VMEM((half, w), f32) for w in wide],
+        *[pltpu.VMEM((LANES, piece, w), f32) for w in wide],
+        *[pltpu.VMEM((width, w), f32) for w in wide],
+        dma((4,)),
+        dma((4, steps, devices)),
+        dma((steps, devices)),
+        dma((steps,)),
+        dma((steps,)),
+        dma((steps, LANES)),
+        dma((steps, LANES)),
+        dma((steps, LANES)),
+        dma((steps, LANES)),
+        dma((steps,)),
+        dma((steps,)),
+    ]
+    whole = pl.BlockSpec(memory_space=pl.ANY)
+    vmem = pl.BlockSpec(memory_space=pltpu.VMEM)
+    return pl.pallas_call(
+        functools.partial(fused_kernel, steps, width),
+        out_shape=(
+            jax.ShapeDtypeStruct((rows, all_cols), f32),
+            jax.ShapeDtypeStruct((all_cols, all_cols), f32),
+        ),
+        in_specs=[whole, whole, whole, whole, pl.BlockSpec(memory_space=pltpu.SMEM)],
+        out_specs=(vmem, vmem),
+        scratch_shapes=scratch,
+        compiler_params=pltpu.CompilerParams(
+            collective_id=0, has_side_effects=True, vmem_limit_bytes=62 * 2**20
+        ),
+    )(anc_inverse, anc_factor, win_factor, pivot_inverse, structure)
+
 
 precise = lax.Precision.HIGHEST
 
@@ -13,6 +379,8 @@
 def on_device(anc_inverse, anc_factor, win_factor, pivot_inverse, structure):
     row_count = lax.axis_size("prow")
     col_count = lax.axis_size("pcol")
+    if row_count == 1 and col_count == 4 * Z and 2 * anc_factor.shape[0] == 3 * pivot_inverse.shape[1]:
+        return fused(anc_inverse, anc_factor, win_factor, pivot_inverse, structure)
     row_index = lax.axis_index("prow")
     col_index = lax.axis_index("pcol")
     block_rows = anc_inverse.shape[0]

time: 906 us -> 157 us (0.17)
  waiting for transfers between devices: 773 us -> 0 us
  Pallas kernels: 0 us -> 152 us
  matrix products: 80.8 us -> 0 us
  other arithmetic: 21.5 us -> 0 us
  between operations: 14.3 us -> 0.65 us
    reduce_scatter x3 -> x0, waiting for transfers between devices: 551 us -> none  [on_device(): lax.psum_scatter(term_rows(jnp.int32(0), share_rows * lax.axis_size('pcol...]
    pallas_call x0 -> x1, Pallas kernels: none -> 152 us  [fused(): pl.pallas_call(functools.partial(fused_kernel, steps, width), out_shape=(...]
    all_gather x2 -> x0, waiting for transfers between devices: 130 us -> none  [on_device(): column_now = lax.all_gather(share_column, 'pcol', axis=0, tiled=True)]
    psum x1 -> x0, waiting for transfers between devices: 91.5 us -> none  [on_device(): pivot_sum = lax.psum(pivot_part, ('prow', 'pcol'))]
    dot_general x20 -> x0, matrix products: 80.8 us -> none  [product(): jnp.dot(left, right, precision=precise, preferred_element_type=jnp.float32)]
  transfers between devices with their start and end apart: 7 -> 0, of which waited for: 6 -> 0; matrix products, arithmetic and copies ran while one was open for 6% -> 0% of each run, Pallas kernels for 0% -> 0%
where the time goes in v1:
time: 157 us
  Pallas kernels  152 us (97%)
  local copies, waits for them, and re-layouts  3.92 us (2%)
    pallas_call x1, Pallas kernels, fused(): pl.pallas_call(functools.partial(fused_kernel, steps, width), out_shape=(...  152 us
    unnamed x4, local copies, waits for them, and re-layouts  3.92 us

profile of v1, /device:TPU:1, one launch (start us, length us, event | category | flops | bytes accessed | tf_op | source)
XLA Modules:
  0.0 156.9 jit_solution(6992424253158364685)
XLA Ops:
  0.6 152.3 %shard_map.68 = (f32[384,768]{1,0:T(8,128)}, f32[768,768]{1,0:T(8,128)}) custom-call(f32[6144,384]{1,0:T(8,128)} %anc_ref.1, f32[384,768]{1,0:T(8,128)} %fac_ref.1, f32[768,768]{1,0:T(8,128)} %win_ref.1, f32[3,256,256]{2,1,0:T(8,128)} %piv_ref.1, s32[3,24]{1,0:T(4,128)} %str_ref.1), custom_call_target="tpu_custom_call" | custom-call | tf_op jit(solution)/shard_map/pallas_call | solution.py:357
  153.0 0.0 copy-start
  153.0 2.5 %copy.9 = f32[384,768]{1,0:T(8,128)} copy(f32[384,768]{1,0:T(8,128)} %get-tuple-element.4) | data formatting | bytes 2359296
  155.5 0.0 copy-done
  155.5 1.4 copy.10
Async XLA Ops:
  153.0 2.5 %copy-start = (f32[768,768]{1,0:T(8,128)S(1)}, f32[768,768]{1,0:T(8,128)}, u32[]{:S(2)}) copy-start(f32[768,768]{1,0:T(8,128)} %get-tuple-element.5) | copy-start | bytes 7077892

commit v2 on v1

--- a/solution.py
+++ b/solution.py
@@ -148,17 +148,17 @@
             return carry
 
         if t == 0:
-            acc[...] = jnp.zeros_like(acc)
+            start = jnp.zeros(acc.shape, jnp.float32)
+            for j in range(k + 1, steps):
+                start = start + mul(cols_ref[:, j * width : (j + 1) * width], fac_block(j, k))
+            acc[...] = start
         lax.fori_loop(0, 4, body, 0)
 
     def fac_block(j, k):
         return win_st[j * width : (j + 1) * width, k * width : (k + 1) * width]
 
     def finish(k):
-        total = acc[...]
-        for j in range(k + 1, steps):
-            total = total + mul(cols_ref[:, j * width : (j + 1) * width], fac_block(j, k))
-        column = -total
+        column = -acc[...]
         cols_ref[:, k * width : (k + 1) * width] = column
         flipped = split(column.T)
         for i in range(k + 1):
@@ -290,7 +290,7 @@
             across_event(*events[g - lag_across])
         for k, first in pending:
             number = g - first + 1
-            if 2 <= number <= 5:
+            if 2 <= number <= (5 if k > 1 else 4):
                 phase(k, number)
         if g >= lag_compute:
             k, t = events[g - lag_compute]
@@ -299,11 +299,10 @@
                 finish(k)
                 phase(k, 1)
                 pending.append((k, g))
-    for g in range(len(events) + lag_compute, len(events) + lag_compute + 4):
-        for k, first in pending:
-            number = g - first + 1
-            if 2 <= number <= 5:
-                phase(k, number)
+    phase(0, 2)
+    phase(1, 5)
+    for number in range(3, 6):
+        phase(0, number)
 
     for k, t in events:
         column_sends(k, t, lambda copy: copy.wait_send())

time: 157 us -> 155 us (0.987)
  Pallas kernels: 152 us -> 150 us
    pallas_call x1, Pallas kernels: 152 us -> 150 us  [fused(): pl.pallas_call(functools.partial(fused_kernel, steps, width), out_shape=(...]
where the time goes in v2:
time: 155 us
  Pallas kernels  150 us (97%)
  local copies, waits for them, and re-layouts  3.92 us (3%)
    pallas_call x1, Pallas kernels, fused(): pl.pallas_call(functools.partial(fused_kernel, steps, width), out_shape=(...  150 us
    unnamed x4, local copies, waits for them, and re-layouts  3.92 us

profile of v2, /device:TPU:1, one launch (start us, length us, event | category | flops | bytes accessed | tf_op | source)
XLA Modules:
  0.0 154.5 jit_solution(2086743151327012805)
XLA Ops:
  0.6 149.9 %shard_map.68 = (f32[384,768]{1,0:T(8,128)}, f32[768,768]{1,0:T(8,128)}) custom-call(f32[6144,384]{1,0:T(8,128)} %anc_ref.1, f32[384,768]{1,0:T(8,128)} %fac_ref.1, f32[768,768]{1,0:T(8,128)} %win_ref.1, f32[3,256,256]{2,1,0:T(8,128)} %piv_ref.1, s32[3,24]{1,0:T(4,128)} %str_ref.1), custom_call_target="tpu_custom_call" | custom-call | tf_op jit(solution)/shard_map/pallas_call | solution.py:356
  150.6 0.0 copy-start
  150.6 2.5 %copy.9 = f32[384,768]{1,0:T(8,128)} copy(f32[384,768]{1,0:T(8,128)} %get-tuple-element.4) | data formatting | bytes 2359296
  153.1 0.0 copy-done
  153.1 1.4 copy.10
Async XLA Ops:
  150.6 2.5 %copy-start = (f32[768,768]{1,0:T(8,128)S(1)}, f32[768,768]{1,0:T(8,128)}, u32[]{:S(2)}) copy-start(f32[768,768]{1,0:T(8,128)} %get-tuple-element.5) | copy-start | bytes 7077892
